TPU v7x, 32 devices: a whole 2x2x4 slice. The times are simulated.
32 devices in a mesh: wave: 4 (over z), tile: 8 (over y, x, core).
Axes of the slice: x: 2, y: 2, z: 4, core: 2. Of those that a mesh axis runs over, the one named last changes fastest.
Arguments:
- hit_energy: bfloat16 [1024, 32, 128], P('tile', 'wave'), may hold values from -24 to 24
- hit_spot: int32 [4, 1024, 128], P('wave', 'tile'), may hold values from 0 to 511
- block_tile: int32 [4, 1024, 1], P('wave', 'tile'), may hold values from 0 to 7; in each aligned block of 128 rows (0 to 127, 128 to 255, ..., all dimensions but the last counted through in order) at most 32 rows name the same one
- block_count: int32 [4, 1024], P('wave', 'tile'), may hold values from 64 to 128
- block_scene: int32 [4, 1024], P('wave', 'tile'), may hold values from 0 to 3
- block_row: int32 [4, 1024], P('wave', 'tile'), may hold values from 0 to 12
- psf_bank: float32 [64, 32, 961], P(None, 'wave'), may hold values from 0 to 0.004162331
- psf_index: int32 [8, 4, 1], P('tile'), may hold values from 0 to 63
- response: float32 [32, 3], replicated, may hold values from -1 to 1
- conv_in: bfloat16 [64, 3, 3, 3], replicated, may hold values from -1.25 to 1.25
- conv_out: bfloat16 [64, 64, 3, 3], replicated, may hold values from -0.25 to 0.25
Outputs:
- features: bfloat16 [4, 64, 128, 128], P('wave', None, 'tile')
Inputs may be any that keep to these rules, and one draw needn't show every extreme that they name: `block_tile`: among the 128 blocks of one device at most 32 name the same tile, a bound that some device reaches.
All inputs are finite; a program needn't handle non-finite values.
Results may differ from a plain program's by a relative error of at most 0.0058.
Values may be sent and summed in bfloat16 or wider, within the bound.
A program may use at most 64 MiB of HBM per device.

v0:
```python
import math

import jax
import jax.numpy as jnp
from jax import lax
from jax.sharding import PartitionSpec as P

ROWS_DEV = 16
W = 128
WIN = 4
K = 31


def padded_2(cells, sides, width):
    for axis, dim in sides:
        count = lax.axis_size(axis)
        ends = count - 1
        head = lax.slice_in_dim(cells, 0, width, axis=dim)
        tail = lax.slice_in_dim(cells, cells.shape[dim] - width, cells.shape[dim], axis=dim)
        cells = jnp.concatenate(
            [
                lax.ppermute(tail, axis, [(i, (i + 1) % count) for i in range(ends)]),
                cells,
                lax.ppermute(head, axis, [((i + 1) % count, i) for i in range(ends)]),
            ],
            axis=dim,
        )
    return cells


def conv_rows(image, weights):
    return lax.conv_general_dilated(
        image,
        weights,
        (1, 1),
        ((0, 0), (1, 1)),
        dimension_numbers=("NCHW", "OIHW", "NCHW"),
        preferred_element_type=jnp.float32,
    )


def patch_blur(extended, psf_bank, psf_index, radius):
    band_dev, scenes, tall, width = extended.shape
    rows_dev = tall - 2 * radius
    patch_count = psf_index.shape[2]
    patch_width = width // patch_count
    side = 2 * radius + 1
    channels = band_dev * scenes * patch_count
    padded = jnp.pad(extended, ((0, 0), (0, 0), (0, 0), (radius, radius)))
    pieces = jnp.stack([padded], axis=2)
    stacked = pieces.reshape(1, channels, tall, patch_width + 2 * radius)
    bank_count = psf_bank.shape[0]
    chosen = (
        psf_index.reshape(-1)[:, None] == jnp.arange(bank_count, dtype=jnp.int32)[None, :]
    ).astype(jnp.float32)
    kernels = jnp.dot(chosen, psf_bank.reshape(bank_count, -1), precision=lax.Precision.HIGHEST)
    kernels = (
        kernels.reshape(scenes, patch_count, band_dev, side, side)
        .transpose(2, 0, 1, 3, 4)
        .reshape(channels, 1, side, side)
    )
    blurred = lax.conv_general_dilated(
        stacked,
        kernels,
        (1, 1),
        "VALID",
        dimension_numbers=("NCHW", "OIHW", "NCHW"),
        feature_group_count=channels,
        precision=lax.Precision.HIGHEST,
    )
    blurred = blurred.reshape(band_dev, scenes, patch_count, rows_dev, patch_width).transpose(
        0, 1, 3, 2, 4
    )
    return blurred.reshape(band_dev, scenes, rows_dev, width)


def window_splat(energy, spots, bases, scenes):
    slots, band_dev, hit_lanes = energy.shape
    group_size = math.gcd(slots, 128)
    steps_total = slots // group_size
    span = WIN * W
    row_total = scenes * ROWS_DEV
    energy = energy.reshape(steps_total, group_size, band_dev, hit_lanes)
    spots = spots.reshape(steps_total, group_size, hit_lanes)
    bases = bases.reshape(steps_total, group_size)
    positions = jnp.arange(span, dtype=jnp.int32)
    offsets = jnp.arange(WIN, dtype=jnp.int32)
    row_ids = jnp.arange(row_total, dtype=jnp.int32)

    def add_group(total, pieces):
        part_energy, part_spot, part_base = pieces
        onehot = (part_spot[:, :, None] == positions[None, None, :]).astype(part_energy.dtype)
        window = jnp.einsum("ibh,ihp->ibp", part_energy, onehot, preferred_element_type=jnp.float32)
        window = window.reshape(group_size, band_dev, WIN, W)
        placing = (
            part_base[:, None, None] + offsets[None, :, None] == row_ids[None, None, :]
        ).astype(jnp.float32)
        added = jnp.einsum("ibjx,ijr->brx", window, placing, precision=lax.Precision.HIGHEST)
        return (total + added, None)

    start = jnp.zeros((band_dev, row_total, W), jnp.float32)
    total, unused = lax.scan(add_group, start, (energy, spots, bases))
    return total.reshape(band_dev, scenes, ROWS_DEV, W)


def per_device(
    hit_energy,
    hit_spot,
    block_tile,
    block_count,
    block_scene,
    block_row,
    psf_bank,
    psf_index,
    response,
    conv_in,
    conv_out,
):
    tile_count = lax.axis_size("tile")
    block_dev, band_dev, hit_lanes = hit_energy.shape
    capacity = 2 * block_dev // tile_count
    scenes = psf_index.shape[1]
    lanes = lax.broadcasted_iota(jnp.int32, (block_dev, hit_lanes), 1)
    live = lanes < block_count[0][:, None]
    masked = jnp.where(live[:, None, :], hit_energy, jnp.zeros_like(hit_energy))
    base_row = block_scene[0] * ROWS_DEV + block_row[0]
    target = block_tile[0, :, 0]
    owners = (target[:, None] == jnp.arange(tile_count, dtype=jnp.int32)[None, :]).astype(jnp.int32)
    before = jnp.cumsum(owners, axis=0) - owners
    place = target * capacity + jnp.sum(before * owners, axis=1)
    send_energy = (
        jnp.zeros((tile_count * capacity, band_dev, hit_lanes), hit_energy.dtype)
        .at[place]
        .set(masked)
    )
    send_spot = jnp.zeros((tile_count * capacity, hit_lanes), jnp.int32).at[place].set(hit_spot[0])
    send_base = jnp.zeros((tile_count * capacity,), jnp.int32).at[place].set(base_row)
    got_energy, got_spot, got_base = (
        lax.all_to_all(send_energy, "tile", split_axis=0, concat_axis=0, tiled=True),
        lax.all_to_all(send_spot, "tile", split_axis=0, concat_axis=0, tiled=True),
        lax.all_to_all(send_base, "tile", split_axis=0, concat_axis=0, tiled=True),
    )
    splat = window_splat(got_energy, got_spot, got_base, scenes)
    extended = padded_2(splat, (("tile", 2),), K // 2)
    blurred = patch_blur(extended, psf_bank, psf_index, K // 2)
    gathered = lax.all_to_all(blurred, "wave", split_axis=1, concat_axis=0, tiled=True)
    color = jnp.einsum("bsyx,bc->scyx", gathered, response, precision=lax.Precision.HIGHEST)
    sensor = color.astype(jnp.bfloat16)
    rimmed = padded_2(sensor, (("tile", 2),), 2)
    grown = jax.nn.silu(conv_rows(rimmed, conv_in))
    rows_here = (
        lax.broadcasted_iota(jnp.int32, (1, 1, ROWS_DEV + 2, 1), 2)
        + lax.axis_index("tile") * ROWS_DEV
        - 1
    )
    inside = (rows_here >= 0) & (rows_here < ROWS_DEV * tile_count)
    hidden_rimmed = jnp.where(inside, grown, jnp.zeros_like(grown)).astype(jnp.bfloat16)
    return conv_rows(hidden_rimmed, conv_out).astype(jnp.bfloat16)


def solution(mesh):
    in_specs = (
        P("tile", "wave", None),
        P("wave", "tile", None),
        P("wave", "tile", None),
        P("wave", "tile"),
        P("wave", "tile"),
        P("wave", "tile"),
        P(None, "wave", None),
        P("tile", None, None),
        P(),
        P(),
        P(),
    )
    out_specs = P("wave", None, "tile", None)
    return jax.shard_map(
        per_device, mesh=mesh, in_specs=in_specs, out_specs=out_specs, check_vma=False
    )
```

profile of v0, /device:TPU:11, one launch (start us, length us, event | category | flops | bytes accessed | tf_op | source)
XLA Modules:
  0.0 209.1 jit_solution(9862912881551560051)
XLA Ops:
  0.0 0.8 fusion.54
  0.8 0.2 reduce_window_sum.11
  1.0 0.8 select_reduce_fusion
  1.8 0.7 fusion.60
  2.5 0.7 add_bitcast_fusion
  3.1 1.0 scatter_custom_fusion
  4.1 0.7 all_to_all.26
  4.8 4.6 %all-to-all-start = ((s32[8,32,1]{1,2,0:T(1,128)}), s32[8,32,1]{1,2,0:T(1,128)S(1)}, u32[]{:S(2)}, u32[]{:S(2)}) async-start(s32[8,32,1]{1,2,0:T(1,128)} %all_to_all.26), calls=%async_computation | async-start | bytes 8192 | tf_op jit(solution)/shard_map/all_to_all | solution.py:141
  9.4 0.7 iota_compare_fusion.10
  10.1 1.8 scatter_custom_fusion.2
  11.9 0.2 all-to-all-done
  12.1 5.2 %all-to-all-start.2 = ((s32[8,32,128]{2,1,0:T(8,128)}), s32[8,32,128]{2,1,0:T(8,128)S(1)}, u32[]{:S(2)}, u32[]{:S(2)}) async-start(s32[8,32,128]{2,1,0:T(8,128)} %bitcast.8), calls=%async_computation.2 | async-start | bytes 262144 | tf_op jit(solution)/shard_map/all_to_all | solution.py:140
  17.3 1.0 broadcast_select_fusion
  18.3 0.9 broadcast_in_dim.48
  19.2 12.5 %scatter_fusion = bf16[256,8,128]{2,1,0:T(8,128)(2,1)} fusion(bf16[256,8,128]{2,1,0:T(8,128)(2,1)} %broadcast_in_dim.48, s32[128]{0:T(128)S(1)} %fusion.60, bf16[128,8,128]{2,1,0:T(8,128)(2,1)S(1)} %broadcast_select_fusion), kind=kCustom, calls=%fused_computation.1 | custom fusion | bytes 786944 | tf_op jit(solution)/shard_map/scatter | solution.py:134
  31.7 4.2 %all-to-all-start.1 = ((bf16[256,8,128]{2,1,0:T(8,128)(2,1)}), bf16[256,8,128]{2,1,0:T(8,128)(2,1)S(1)}, u32[]{:S(2)}, u32[]{:S(2)}) async-start(bf16[256,8,128]{2,1,0:T(8,128)(2,1)} %scatter_fusion), calls=%async_computation.1 | async-start | bytes 1048576 | tf_op jit(solution)/shard_map/all_to_all | solution.py:139
  35.9 2.5 %reshape.151 = f32[64,7688]{1,0:T(8,128)S(1)} reshape(f32[64,8,961]{2,1,0:T(8,128)} %param.19) | data formatting | bytes 3936256 | tf_op jit(solution)/shard_map/reshape | solution.py:56
  38.4 2.8 %copy.50 = f32[64,7688]{0,1:T(8,128)} copy(f32[64,7688]{1,0:T(8,128)S(1)} %reshape.151) | data formatting | bytes 3936256 | tf_op jit(solution)/shard_map/reshape | solution.py:56
  41.1 4.8 %reshape.152 = f32[8,31,31,64]{3,2,1,0:T(8,128)} reshape(f32[7688,64]{1,0:T(8,128)} %bitcast.102) | data formatting | bytes 3936256 | tf_op jit(solution)/shard_map/reshape.62
  46.0 0.5 broadcast.172
  46.5 0.6 reduce.3
  47.1 20.3 %while.11 = (s32[]{:T(128)}, f32[8,64,128]{2,1,0:T(8,128)S(1)}, s32[2,128]{1,0:T(2,128)S(1)}, bf16[2,128,8,128]{3,2,1,0:T(8,128)(2,1)S(1)}, s32[2,128,128]{2,1,0:T(8,128)S(1)}, /*index=5*/s32[]{:T(128)}, s32[]{:T(128)}) while((s32[]{:T(128)}, f32[8,64,128]{2,1,0:T(8,128)S(1)}, s32[2,128]{1,0:T(2,128)S(1)}, ...), condition=%wide.region_6.7_spmd.clone, body=%wide.region_5.6_spmd.clone.sunk | while | flops 545423872 | bytes 5183083 | solution.py:102
  47.2 7.9 %fusion.87 = f32[128,8,4,128]{3,1,2,0:T(8,128)S(1)} fusion(s32[128,128]{1,0:T(8,128)S(1)} %dynamic-slice_bitcast_fusion.2, bf16[2,128,8,128]{3,2,1,0:T(8,128)(2,1)S(1)} %get-tuple-element.136, s32[]{:T(128)S(6)} %copy.84), kind=kOutput, calls=%fused_computation.11.clone.1 | convolution fusion | flops 142606336 | bytes 2424836 | tf_op jit(solution)/shard_map/while/body/eval_jaxpr/ibh,ihp->ibp/dot_general | solution.py:93
  55.1 2.1 %fusion.89 = f32[8,64,128]{2,1,0:T(8,128)S(1)} fusion(f32[128,8,4,128]{3,1,2,0:T(8,128)S(1)} %fusion.87, f32[8,64,128]{2,1,0:T(8,128)S(1)} %get-tuple-element.127, pred[]{:T(512)S(6)} %compare.46, s32[128,4]{0,1:T(4,128)S(1)} %iota_add_fusion.2), kind=kOutput, calls=%fused_computation.13.clone.1 | convolution fusion | flops 402817024 | bytes 2623489 | tf_op jit(solution)/shard_map/while/body/eval_jaxpr/ibjx,ijr->brx/dot_general | solution.py:98
  57.3 7.9 %fusion.87 = f32[128,8,4,128]{3,1,2,0:T(8,128)S(1)} fusion(s32[128,128]{1,0:T(8,128)S(1)} %dynamic-slice_bitcast_fusion.2, bf16[2,128,8,128]{3,2,1,0:T(8,128)(2,1)S(1)} %get-tuple-element.136, s32[]{:T(128)S(6)} %copy.84), kind=kOutput, calls=%fused_computation.11.clone.1 | convolution fusion | flops 142606336 | bytes 2424836 | tf_op jit(solution)/shard_map/while/body/eval_jaxpr/ibh,ihp->ibp/dot_general | solution.py:93
  65.3 2.1 %fusion.89 = f32[8,64,128]{2,1,0:T(8,128)S(1)} fusion(f32[128,8,4,128]{3,1,2,0:T(8,128)S(1)} %fusion.87, f32[8,64,128]{2,1,0:T(8,128)S(1)} %get-tuple-element.127, pred[]{:T(512)S(6)} %compare.46, s32[128,4]{0,1:T(4,128)S(1)} %iota_add_fusion.2), kind=kOutput, calls=%fused_computation.13.clone.1 | convolution fusion | flops 402817024 | bytes 2623489 | tf_op jit(solution)/shard_map/while/body/eval_jaxpr/ibjx,ijr->brx/dot_general | solution.py:98
  67.5 3.3 %collective-permute-start = (f32[8,4,15,128]{3,2,1,0:T(8,128)S(1)}, f32[8,4,15,128]{3,2,1,0:T(8,128)S(1)}, u32[]{:S(2)}, u32[]{:S(2)}) collective-permute-start(f32[8,4,15,128]{3,2,1,0:T(8,128)S(1)} %get-tuple-element.84), channel_id=1, source_target_pairs={{0,1},{1,2},{2,3},{3,4},{4,5},{5,6},{6,7},{8,9},{9,10},{10,11},{11... | collective-permute-start | bytes 737288 | tf_op jit(solution)/shard_map/ppermute | solution.py:22
  70.8 1.9 collective-permute-start.1
  72.7 10.1 %convolution_bitcast_fusion = f32[8,4,1,31,31]{4,1,3,0,2:T(4,128)S(1)} fusion(f32[8,31,31,64]{3,2,1,0:T(8,128)} %reshape.152, s32[4]{0:T(128)S(1)} %bitcast.112), kind=kOutput, calls=%fused_computation.36 | convolution fusion | flops 23617792 | bytes 2091152 | tf_op jit(solution)/shard_map/dot_general | solution.py:56
  82.9 0.2 copy.51
  83.0 1.4 copy.53
  84.4 0.6 select_maximum_fusion
  85.1 6.3 %copy.52 = f32[1,32,46,158]{1,0,3,2:T(1,128)} copy(f32[1,32,46,158]{3,2,1,0:T(8,128)S(1)} %bitcast.103) | data formatting | bytes 1860608 | tf_op jit(solution)/shard_map/reshape;stack | solution.py:51
  91.3 88.4 %fusion.73 = f32[1,32,16,128]{1,0,3,2:T(1,128)S(1)} fusion(f32[1,32,46,158]{1,0,3,2:T(1,128)} %copy.52, f32[32,1,31,31]{0,1,3,2:T(1,128)S(1)} %copy.53), kind=kOutput, calls=%fused_computation.92 | convolution fusion | flops 755761152 | bytes 1315456 | tf_op jit(solution)/shard_map/conv_general_dilated | solution.py:62
  179.8 0.5 copy.54
  180.3 0.7 copy.55
  181.0 4.8 %all-to-all-start.3 = ((f32[8,4,16,128]{3,2,0,1:T(8,128)}), f32[8,4,16,128]{3,2,0,1:T(8,128)S(1)}, u32[]{:S(2)}, u32[]{:S(2)}) async-start(f32[8,4,16,128]{3,2,0,1:T(8,128)} %copy.55), calls=%async_computation.3 | async-start | bytes 524288 | tf_op jit(solution)/shard_map/all_to_all | solution.py:146
  185.8 6.1 %all-to-all-done.3 = f32[8,4,16,128]{3,2,0,1:T(8,128)S(1)} async-done(((f32[8,4,16,128]{3,2,0,1:T(8,128)}), f32[8,4,16,128]{3,2,0,1:T(8,128)S(1)}, u32[]{:S(2)}, u32[]{:S(2)}) %all-to-all-start.3) | async-done | bytes 262176 | tf_op jit(solution)/shard_map/all_to_all | solution.py:146
  191.9 0.3 fusion.29
  192.2 5.3 %collective-permute-start.2 = (bf16[1,3,2,128]{3,1,2,0:T(4,128)(2,1)S(1)}, bf16[1,3,2,128]{3,1,2,0:T(4,128)(2,1)S(1)}, u32[]{:S(2)}, u32[]{:S(2)}) collective-permute-start(bf16[1,3,2,128]{3,1,2,0:T(4,128)(2,1)S(1)} %get-tuple-element.86), channel_id=1, source_target_pairs={{0,1},{1,2},{2,3},{3,4},{4,5},{5,6},{6,7},{8,9},{9,10},{10,11},{11... | collective-permute-start | bytes 4616 | tf_op jit(solution)/shard_map/ppermute | solution.py:22
  197.6 1.9 collective-permute-start.3
  199.5 3.8 %collective-permute-done.3 = bf16[1,3,2,128]{3,1,2,0:T(4,128)(2,1)S(1)} collective-permute-done((bf16[1,3,2,128]{3,1,2,0:T(4,128)(2,1)S(1)}, bf16[1,3,2,128]{3,1,2,0:T(4,128)(2,1)S(1)}, u32[]{:S(2)}, u32[]{:S(2)}) %collective-permute-start.3) | collective-permute-done | bytes 1568 | tf_op jit(solution)/shard_map/ppermute | solution.py:24
  203.5 0.1 reshape.198
  203.6 0.6 copy.59
  204.2 0.1 slice.24
  204.3 1.4 fusion.28
  205.8 1.5 convolution_convert_fusion
  207.4 1.3 copy.62
  (31 shorter events, 0.5 us)
Async XLA Ops:
  0.0 205.8 %copy-start = (bf16[64,64,3,3]{1,0,3,2:T(8,128)(2,1)S(1)}, bf16[64,64,3,3]{1,0,3,2:T(8,128)(2,1)}, u32[]{:S(2)}) copy-start(bf16[64,64,3,3]{1,0,3,2:T(8,128)(2,1)} %param.23) | copy-start | bytes 221188
  4.8 7.3 %all-to-all-start = ((s32[8,32,1]{1,2,0:T(1,128)}), s32[8,32,1]{1,2,0:T(1,128)S(1)}, u32[]{:S(2)}, u32[]{:S(2)}) async-start(s32[8,32,1]{1,2,0:T(1,128)} %all_to_all.26), calls=%async_computation | async-start | bytes 8192 | tf_op jit(solution)/shard_map/all_to_all | solution.py:141
  12.1 19.6 %all-to-all-start.2 = ((s32[8,32,128]{2,1,0:T(8,128)}), s32[8,32,128]{2,1,0:T(8,128)S(1)}, u32[]{:S(2)}, u32[]{:S(2)}) async-start(s32[8,32,128]{2,1,0:T(8,128)} %bitcast.8), calls=%async_computation.2 | async-start | bytes 262144 | tf_op jit(solution)/shard_map/all_to_all | solution.py:140
  31.7 15.4 %all-to-all-start.1 = ((bf16[256,8,128]{2,1,0:T(8,128)(2,1)}), bf16[256,8,128]{2,1,0:T(8,128)(2,1)S(1)}, u32[]{:S(2)}, u32[]{:S(2)}) async-start(bf16[256,8,128]{2,1,0:T(8,128)(2,1)} %scatter_fusion), calls=%async_computation.1 | async-start | bytes 1048576 | tf_op jit(solution)/shard_map/all_to_all | solution.py:139
  47.1 25.6 %copy-start.2 = (s32[1,4,1]{1,2,0:T(1,128)S(1)}, s32[1,4,1]{1,2,0:T(1,128)}, u32[]{:S(2)}) copy-start(s32[1,4,1]{1,2,0:T(1,128)} %param.20) | copy-start | bytes 52
  67.5 17.0 %collective-permute-start = (f32[8,4,15,128]{3,2,1,0:T(8,128)S(1)}, f32[8,4,15,128]{3,2,1,0:T(8,128)S(1)}, u32[]{:S(2)}, u32[]{:S(2)}) collective-permute-start(f32[8,4,15,128]{3,2,1,0:T(8,128)S(1)} %get-tuple-element.84), channel_id=1, source_target_pairs={{0,1},{1,2},{2,3},{3,4},{4,5},{5,6},{6,7},{8,9},{9,10},{10,11},{11... | collective-permute-start | bytes 737288 | tf_op jit(solution)/shard_map/ppermute | solution.py:22
  70.8 13.6 %collective-permute-start.1 = (f32[8,4,15,128]{3,2,1,0:T(8,128)S(1)}, f32[8,4,15,128]{3,2,1,0:T(8,128)S(1)}, u32[]{:S(2)}, u32[]{:S(2)}) collective-permute-start(f32[8,4,15,128]{3,2,1,0:T(8,128)S(1)} %get-tuple-element.85), channel_id=1, source_target_pairs={{1,0},{2,1},{3,2},{4,3},{5,4},{6,5},{7,6},{9,8},{10,9},{11,10},{12... | collective-permute-start | bytes 737288 | tf_op jit(solution)/shard_map/ppermute | solution.py:24
  179.8 12.1 %copy-start.1 = (f32[32,3]{0,1:T(4,128)S(1)}, f32[32,3]{0,1:T(4,128)}, u32[]{:S(2)}) copy-start(f32[32,3]{0,1:T(4,128)} %param.21) | copy-start | bytes 1156
  179.8 24.5 %copy-start.3 = (bf16[64,3,3,3]{0,3,2,1:T(4,128)(2,1)S(1)}, bf16[64,3,3,3]{0,3,2,1:T(4,128)(2,1)}, u32[]{:S(2)}) copy-start(bf16[64,3,3,3]{0,3,2,1:T(4,128)(2,1)} %param.22) | copy-start | bytes 10372
  179.8 24.5 %copy-start.4 = (pred[8,17]{0,1:T(8,128)(4,1)S(1)}, pred[8,17]{0,1:T(8,128)(4,1)}, u32[]{:S(2)}) copy-start(pred[8,17]{0,1:T(8,128)(4,1)} %constant.64) | copy-start | bytes 412
  181.0 10.9 %all-to-all-start.3 = ((f32[8,4,16,128]{3,2,0,1:T(8,128)}), f32[8,4,16,128]{3,2,0,1:T(8,128)S(1)}, u32[]{:S(2)}, u32[]{:S(2)}) async-start(f32[8,4,16,128]{3,2,0,1:T(8,128)} %copy.55), calls=%async_computation.3 | async-start | bytes 524288 | tf_op jit(solution)/shard_map/all_to_all | solution.py:146
  192.2 7.3 %collective-permute-start.2 = (bf16[1,3,2,128]{3,1,2,0:T(4,128)(2,1)S(1)}, bf16[1,3,2,128]{3,1,2,0:T(4,128)(2,1)S(1)}, u32[]{:S(2)}, u32[]{:S(2)}) collective-permute-start(bf16[1,3,2,128]{3,1,2,0:T(4,128)(2,1)S(1)} %get-tuple-element.86), channel_id=1, source_target_pairs={{0,1},{1,2},{2,3},{3,4},{4,5},{5,6},{6,7},{8,9},{9,10},{10,11},{11... | collective-permute-start | bytes 4616 | tf_op jit(solution)/shard_map/ppermute | solution.py:22
  197.6 5.8 %collective-permute-start.3 = (bf16[1,3,2,128]{3,1,2,0:T(4,128)(2,1)S(1)}, bf16[1,3,2,128]{3,1,2,0:T(4,128)(2,1)S(1)}, u32[]{:S(2)}, u32[]{:S(2)}) collective-permute-start(bf16[1,3,2,128]{3,1,2,0:T(4,128)(2,1)S(1)} %get-tuple-element.87), channel_id=1, source_target_pairs={{1,0},{2,1},{3,2},{4,3},{5,4},{6,5},{7,6},{9,8},{10,9},{11,10},{12... | collective-permute-start | bytes 4616 | tf_op jit(solution)/shard_map/ppermute | solution.py:24
where the time goes:
time: 213 us; the launch traced here: 209 us
  matrix products  122 us (57%)
  local copies, waits for them, and re-layouts  38.9 us (18%)
  starting transfers between devices  31.3 us (15%)
  waiting for transfers between devices  10.1 us (5%)
  other arithmetic  6.09 us (3%)
    conv_general_dilated x1, matrix products, patch_blur(): lax.conv_general_dilated(stacked, kernels, (1, 1), 'VALID', dimension_num...  88.4 us
    dot_general x2, matrix products, add_group(): jnp.einsum('ibh,ihp->ibp', part_energy, onehot, preferred_element_type=jn...  15.9 us
    scatter x1, local copies, waits for them, and re-layouts, per_device(): send_energy = jnp.zeros((tile_count * capacity, band_dev, hit_lanes), hit...  12.5 us
    dot_general x1, matrix products, patch_blur(): jnp.dot(chosen, psf_bank.reshape(bank_count, -1), precision=lax.Precision...  10.1 us
    ppermute x2, starting transfers between devices, padded_2(): lax.ppermute(tail, axis, [(i, (i + 1) % count) for i in range(ends)])  8.67 us
    another operation x1, local copies, waits for them, and re-layouts, patch_blur(): stacked = pieces.reshape(1, channels, tall, patch_width + 2 * radius)  6.27 us
    all_to_all x1, waiting for transfers between devices, per_device(): lax.all_to_all(blurred, 'wave', split_axis=1, concat_axis=0, tiled=True)  6.09 us
    reshape x2, local copies, waits for them, and re-layouts, patch_blur(): psf_bank.reshape(bank_count, -1)  5.23 us
  transfers between devices with their start and end apart: 8, of which 3 were waited for; matrix products, arithmetic and copies ran while one was open for 19% of the time, Pallas kernels for 0%

commit v1 on v0

v1 whole, which is shorter than its diff:
```python
import functools

import jax
import jax.numpy as jnp
from jax import lax
from jax.experimental import pallas as pl
from jax.experimental.pallas import tpu as pltpu
from jax.sharding import PartitionSpec as P

ROWS = 16
W = 128
WIN = 4
K = 31
RAD = K // 2
PITCH = 32
DEPTH = ROWS * PITCH
MESH = pl.DeviceIdType.MESH
F32 = jnp.float32
BF16 = jnp.bfloat16


def dispatch_kernel(n, cap, inv_ref, energy_ref, pos_ref, meta_ref, got_e, got_p, got_m,
                    out_e, out_p, send_sem, recv_sem, local_sem):
    wave = lax.axis_index("wave")
    me = lax.axis_index("tile")
    barrier = pltpu.get_barrier_semaphore()

    @pl.loop(1, n)
    def _(d):
        pl.semaphore_signal(barrier, inc=1, device_id=(wave, lax.rem(me + d, n)), device_id_type=MESH)

    def pack(peer):
        for j in range(cap):
            i = inv_ref[peer, j]
            out_e[peer, j] = energy_ref[jnp.minimum(i, energy_ref.shape[0] - 1)]
            out_p[peer, j] = pos_ref[i]

    def copies(d):
        peer = lax.rem(me + d, n)
        pairs = ((out_e.at[peer], got_e.at[me]), (out_p.at[peer], got_p.at[me]),
                 (meta_ref.at[peer], got_m.at[me]))
        return [
            pltpu.make_async_remote_copy(
                src_ref=src, dst_ref=dst, send_sem=send_sem.at[k, d], recv_sem=recv_sem.at[k, d],
                device_id=(wave, peer), device_id_type=MESH)
            for k, (src, dst) in enumerate(pairs)
        ]

    pack(lax.rem(me + 1, n))
    pl.semaphore_wait(barrier, n - 1)

    @pl.loop(1, n)
    def _(d):
        for copy in copies(d):
            copy.start()
        pack(lax.rem(me + d + 1, n))

    own = [pltpu.make_async_copy(src, dst, local_sem.at[k]) for k, (src, dst) in enumerate(
        ((out_e.at[me], got_e.at[me]), (out_p.at[me], got_p.at[me]), (meta_ref.at[me], got_m.at[me])))]
    for copy in own:
        copy.start()
    for copy in own:
        copy.wait()

    @pl.loop(1, n)
    def _(d):
        for copy in copies(d):
            copy.wait()


def dispatch(inv, energy, pos, meta):
    n, cap = inv.shape
    bands, lanes = energy.shape[1:]
    vmem = pl.BlockSpec(memory_space=pltpu.VMEM)
    hbm = pl.BlockSpec(memory_space=pl.ANY)
    return pl.pallas_call(
        functools.partial(dispatch_kernel, n, cap),
        out_shape=(
            jax.ShapeDtypeStruct((n, cap, bands, lanes), energy.dtype),
            jax.ShapeDtypeStruct((n, cap, 1, lanes), jnp.int32),
            jax.ShapeDtypeStruct((n, 1, lanes), jnp.int32),
        ),
        in_specs=[pl.BlockSpec(memory_space=pltpu.SMEM), vmem, vmem, vmem],
        out_specs=(hbm, hbm, hbm),
        scratch_shapes=[
            pltpu.VMEM((n, cap, bands, lanes), energy.dtype),
            pltpu.VMEM((n, cap, 1, lanes), jnp.int32),
            pltpu.SemaphoreType.DMA((3, n)),
            pltpu.SemaphoreType.DMA((3, n)),
            pltpu.SemaphoreType.DMA((3,)),
        ],
        compiler_params=pltpu.CompilerParams(
            collective_id=0, has_side_effects=True, vmem_limit_bytes=32 * 2**20),
        name="dispatch",
    )(inv, energy, pos, meta)


def blur_kernel(n, cap, scenes, bands, meta_ref, resp_ref, energy_ref, pos_ref, bank_ref, out_ref,
                acc, kpad, amat):
    me = lax.axis_index("tile")
    wave = lax.axis_index("wave")
    group = 8
    acc[...] = jnp.zeros_like(acc)
    xs = lax.broadcasted_iota(jnp.int32, (W, W), 0)

    def splat_source(d, carry):
        @pl.loop(0, cap // group)
        def _(g):
            windows = []
            for k in range(group):
                j = g * group + k
                pos = pos_ref[d, j]
                row = lax.shift_right_arithmetic(pos, 7)
                col = (W - 1) - (pos & (W - 1))
                onehot = jnp.where(xs == col, 1.0, 0.0).astype(BF16)
                energy = energy_ref[d, j].astype(F32)
                parts = [jnp.where(row == r, energy, 0.0) for r in range(WIN)]
                lhs = jnp.concatenate(parts, axis=0).astype(BF16)
                windows.append(lax.dot_general(
                    lhs, onehot, (((1,), (1,)), ((), ())), preferred_element_type=F32))
            for k in range(group):
                base = pl.multiple_of(meta_ref[d, g * group + k] * bands, bands)
                acc[pl.ds(base, WIN * bands), :] += windows[k]
        return carry

    lax.fori_loop(0, n, splat_source, 0)

    lane = lax.broadcasted_iota(jnp.int32, (bands, W), 1)
    shift_v = lax.broadcasted_iota(jnp.int32, (PITCH, W), 0)
    from_x = lax.broadcasted_iota(jnp.int32, (PITCH, W), 1) - shift_v + RAD
    keep = (from_x >= 0) & (from_x < W) & (shift_v < K)
    kpad[...] = jnp.zeros_like(kpad)

    def scene_step(s, carry):
        for part in range(3):
            other = jnp.clip(me + part - 1, 0, n - 1)
            flat = bank_ref[meta_ref[other, 64 + s]]
            flat = jnp.concatenate([flat, jnp.zeros((bands, 1024 + W - K * K), F32)], axis=1)
            for g in range(8):
                cell = jnp.zeros((bands, W), F32)
                for q in range(4):
                    u = 4 * g + q
                    if u >= K:
                        continue
                    base = K * u // W * W
                    shift = (PITCH * q - (K * u - base)) % (2 * W)
                    piece = flat[:, base:base + 2 * W]
                    if shift:
                        piece = pltpu.roll(piece, shift, 1)
                    hit = (lane >= PITCH * q) & (lane < PITCH * q + K)
                    cell = jnp.where(hit, piece[:, :W], cell)
                kpad[:, 512 + g * W:512 + (g + 1) * W] = cell
            for j in range(ROWS):
                start = 512 + PITCH * (RAD - j + ROWS * (1 - part))
                base = start // W * W
                off = start - base
                piece = kpad[:, base:base + DEPTH + W]
                if off:
                    piece = pltpu.roll(piece, DEPTH + W - off, 1)
                for c4 in range(DEPTH // W):
                    amat[c4, pl.ds(part * ROWS + j, bands, stride=3 * ROWS), :] = (
                        piece[:, c4 * W:(c4 + 1) * W])
        colours = [jnp.zeros((3 * ROWS, W), F32) for _ in range(3)]
        for b in range(bands):
            lhs = jnp.concatenate(
                [amat[c4, b * 3 * ROWS:(b + 1) * 3 * ROWS, :] for c4 in range(DEPTH // W)], axis=1
            ).astype(BF16)
            rows = []
            for r in range(ROWS):
                line = acc[pl.ds((s * ROWS + r) * bands + b, 1), :]
                wide = jnp.broadcast_to(line, (PITCH, W))
                wide = pltpu.roll(wide, W - RAD, 1, stride=1, stride_axis=0)
                rows.append(jnp.where(keep, wide, 0.0).astype(BF16))
            rhs = jnp.concatenate(rows, axis=0)
            blurred = jnp.dot(lhs, rhs, preferred_element_type=F32)
            for c in range(3):
                colours[c] = colours[c] + resp_ref[wave * bands + b, c] * blurred
        for part in range(3):
            for c in range(3):
                out_ref[s, part, c] = colours[c][part * ROWS:(part + 1) * ROWS]
        return carry

    lax.fori_loop(0, scenes, scene_step, 0)


def blur(meta, response, energy, pos, bank, scenes):
    n, cap, bands, lanes = energy.shape
    vmem = pl.BlockSpec(memory_space=pltpu.VMEM)
    smem = pl.BlockSpec(memory_space=pltpu.SMEM)
    return pl.pallas_call(
        functools.partial(blur_kernel, n, cap, scenes, bands),
        out_shape=jax.ShapeDtypeStruct((scenes, 3, 3, ROWS, W), F32),
        in_specs=[smem, smem, vmem, vmem, vmem],
        out_specs=vmem,
        scratch_shapes=[
            pltpu.VMEM((scenes * ROWS * bands, W), F32),
            pltpu.VMEM((bands, 2176), F32),
            pltpu.VMEM((DEPTH // W, bands * 3 * ROWS, W), F32),
        ],
        compiler_params=pltpu.CompilerParams(vmem_limit_bytes=48 * 2**20),
        name="blur",
    )(meta, response, energy, pos, bank)


def finish_kernel(waves, n, col_ref, w1_ref, w2_ref, out_ref, got, mine, rim, sens, hid, outs,
                  send_sem, recv_sem, rim_send, rim_recv):
    wave = lax.axis_index("wave")
    me = lax.axis_index("tile")
    has_up = me > 0
    has_down = me < n - 1
    barrier = pltpu.get_barrier_semaphore()

    def guarded(part, body):
        if part == 0:
            pl.when(has_up)(body)
        elif part == 2:
            pl.when(has_down)(body)
        else:
            body()

    todo = [(dw, part) for dw in range(waves) for part in range(3) if (dw, part) != (0, 1)]
    for dw, part in todo:
        def greet(dw=dw, part=part):
            pl.semaphore_signal(barrier, inc=1,
                                device_id=(lax.rem(wave + dw, waves), me + part - 1), device_id_type=MESH)
        guarded(part, greet)
    sides = jnp.where(has_up, 1, 0) + jnp.where(has_down, 1, 0)
    pl.semaphore_wait(barrier, waves - 1 + waves * sides)

    def copy_of(dw, part):
        scene = lax.rem(wave + dw, waves)
        return pltpu.make_async_remote_copy(
            src_ref=col_ref.at[scene, part], dst_ref=got.at[dw, part],
            send_sem=send_sem.at[dw, part], recv_sem=recv_sem.at[dw, part],
            device_id=(scene, me + part - 1), device_id_type=MESH)

    for dw, part in todo:
        guarded(part, lambda dw=dw, part=part: copy_of(dw, part).start())

    @pl.when(jnp.logical_not(has_down))
    def _():
        for dw in range(waves):
            got[dw, 0] = jnp.zeros(got.shape[2:], F32)
        rim[1] = jnp.zeros(rim.shape[1:], F32)

    @pl.when(jnp.logical_not(has_up))
    def _():
        for dw in range(waves):
            got[dw, 2] = jnp.zeros(got.shape[2:], F32)
        rim[0] = jnp.zeros(rim.shape[1:], F32)

    for dw, part in todo:
        guarded(2 - part, lambda dw=dw, part=part: copy_of(dw, part).wait_recv())
    total = col_ref[wave, 1]
    for dw, part in todo:
        total = total + got[dw, part]
    sensor = total.astype(BF16)
    flip_r = lax.broadcasted_iota(jnp.int32, (W, W), 0)
    flip_c = lax.broadcasted_iota(jnp.int32, (W, W), 1)
    mirror = jnp.where(flip_r + flip_c == W - 1, 1.0, 0.0).astype(BF16)
    plain = jnp.dot(sensor.reshape(3 * ROWS, W), mirror, preferred_element_type=F32)
    mine[...] = plain.reshape(3, ROWS, W)

    def to_down():
        return pltpu.make_async_remote_copy(
            src_ref=mine.at[:, pl.ds(8, 8)], dst_ref=rim.at[0], send_sem=rim_send.at[0],
            recv_sem=rim_recv.at[0], device_id=(wave, me + 1), device_id_type=MESH)

    def to_up():
        return pltpu.make_async_remote_copy(
            src_ref=mine.at[:, pl.ds(0, 8)], dst_ref=rim.at[1], send_sem=rim_send.at[1],
            recv_sem=rim_recv.at[1], device_id=(wave, me - 1), device_id_type=MESH)

    pl.when(has_down)(lambda: to_down().start())
    pl.when(has_up)(lambda: to_up().start())

    sens[...] = jnp.zeros_like(sens)
    for c in range(3):
        sens[pl.ds(2 * 8 + c, ROWS, stride=8), :] = plain[c * ROWS:(c + 1) * ROWS]
    pl.when(has_up)(lambda: to_down().wait_recv())
    pl.when(has_down)(lambda: to_up().wait_recv())
    for c in range(3):
        for k in range(2):
            sens[pl.ds(k * 8 + c, 1), :] = rim[0, c, 6 + k:7 + k]
            sens[pl.ds((ROWS + 2 + k) * 8 + c, 1), :] = rim[1, c, k:k + 1]

    def shifted(values):
        xs = lax.broadcasted_iota(jnp.int32, values.shape, 1)
        left = jnp.where(xs == 0, 0.0, pltpu.roll(values, 1, 1))
        right = jnp.where(xs == W - 1, 0.0, pltpu.roll(values, W - 1, 1))
        return left, values, right

    spread = jnp.concatenate(
        [jnp.concatenate(shifted(sens[y * 8:(y + 1) * 8, :]), axis=0) for y in range(ROWS + 4)], axis=0
    )
    w1 = w1_ref[...]
    for y in range(ROWS + 2):
        rhs = spread[y * 24:(y + 3) * 24].astype(BF16)
        value = jnp.dot(w1, rhs, preferred_element_type=F32)
        value = value / (1.0 + jnp.exp(-value))
        if y == 0:
            value = jnp.where(has_up, value, 0.0)
        if y == ROWS + 1:
            value = jnp.where(has_down, value, 0.0)
        hid[y] = jnp.concatenate(shifted(value), axis=0).astype(BF16)
    w2 = w2_ref[...]
    channels = w2.shape[0]
    for y in range(ROWS):
        rhs = hid[y:y + 3].reshape(9 * channels, W)
        outs[pl.ds(y, channels, stride=ROWS), :] = jnp.dot(w2, rhs, preferred_element_type=F32)
    out_ref[0] = outs[...].reshape(channels, ROWS, W).astype(BF16)

    for dw, part in todo:
        guarded(part, lambda dw=dw, part=part: copy_of(dw, part).wait_send())
    pl.when(has_down)(lambda: to_down().wait_send())
    pl.when(has_up)(lambda: to_up().wait_send())


def finish(col, w1, w2, waves, n):
    channels = w2.shape[0]
    vmem = pl.BlockSpec(memory_space=pltpu.VMEM)
    return pl.pallas_call(
        functools.partial(finish_kernel, waves, n),
        out_shape=jax.ShapeDtypeStruct((1, channels, ROWS, W), BF16),
        in_specs=[vmem] * 3,
        out_specs=vmem,
        scratch_shapes=[
            pltpu.VMEM((waves, 3, 3, ROWS, W), F32),
            pltpu.VMEM((3, ROWS, W), F32),
            pltpu.VMEM((2, 3, 8, W), F32),
            pltpu.VMEM(((ROWS + 4) * 8, W), F32),
            pltpu.VMEM((ROWS + 2, 3 * channels, W), BF16),
            pltpu.VMEM((channels * ROWS, W), F32),
            pltpu.SemaphoreType.DMA((waves, 3)),
            pltpu.SemaphoreType.DMA((waves, 3)),
            pltpu.SemaphoreType.DMA((2,)),
            pltpu.SemaphoreType.DMA((2,)),
        ],
        compiler_params=pltpu.CompilerParams(
            collective_id=1, has_side_effects=True, vmem_limit_bytes=32 * 2**20),
        name="finish",
    )(col, w1, w2)


def per_device(hit_energy, hit_spot, block_tile, block_count, block_scene, block_row, psf_bank,
               psf_index, response, conv_in, conv_out):
    n = lax.axis_size("tile")
    waves = lax.axis_size("wave")
    blocks, bands, lanes = hit_energy.shape
    cap = 2 * blocks // n
    scenes = psf_index.shape[1]
    target = block_tile[0, :, 0]
    base = block_scene[0] * ROWS + block_row[0]
    order = jnp.arange(blocks, dtype=jnp.int32)
    same = (target[:, None] == target[None, :]) & (order[None, :] < order[:, None])
    rank = jnp.sum(same.astype(jnp.int32), axis=1)
    tiles = jnp.arange(n, dtype=jnp.int32)
    slots = jnp.arange(lanes, dtype=jnp.int32)
    here = (target[None, None, :] == tiles[:, None, None]) & (rank[None, None, :] == slots[None, :, None])
    inv = blocks + jnp.sum(jnp.where(here, order - blocks, 0), axis=2)
    bases = jnp.sum(jnp.where(here, base, 0), axis=2)
    psf_row = jnp.pad(psf_index[0, :, 0], (64, lanes - 64 - scenes))
    meta = jnp.where(slots[None, :] < 64, bases, psf_row[None, :])[:, None, :]
    live = slots[None, :] < block_count[0][:, None]
    pos = jnp.where(live, hit_spot[0], -1)
    pos = jnp.concatenate([pos, jnp.full((1, lanes), -1, jnp.int32)], axis=0)[:, None, :]
    got_e, got_p, got_m = dispatch(inv[:, :cap], hit_energy, pos, meta)
    col = blur(got_m[:, 0, :], response, got_e, got_p, psf_bank, scenes)
    w1 = jnp.pad(conv_in.transpose(0, 2, 3, 1), ((0, 0), (0, 0), (0, 0), (0, 5))).reshape(-1, 72)
    w2 = conv_out.transpose(0, 2, 3, 1).reshape(conv_out.shape[0], -1)
    return finish(col, w1, w2, waves, n)


def solution(mesh):
    in_specs = (
        P("tile", "wave", None),
        P("wave", "tile", None),
        P("wave", "tile", None),
        P("wave", "tile"),
        P("wave", "tile"),
        P("wave", "tile"),
        P(None, "wave", None),
        P("tile", None, None),
        P(),
        P(),
        P(),
    )
    out_specs = P("wave", None, "tile", None)
    return jax.shard_map(
        per_device, mesh=mesh, in_specs=in_specs, out_specs=out_specs, check_vma=False
    )
```

time: 213 us -> 50.3 us (0.24); the launches traced: 209 us -> 50 us
  matrix products: 122 us -> 0 us
  Pallas kernels: 0 us -> 41.1 us
  local copies, waits for them, and re-layouts: 38.9 us -> 5.2 us
  starting transfers between devices: 31.3 us -> 0 us
  waiting for transfers between devices: 10.1 us -> 0 us
  other arithmetic: 6.09 us -> 3.54 us
    conv_general_dilated x3 -> x0, matrix products: 91.3 us -> none  [the longest x1 88.4 us: patch_blur(): lax.conv_general_dilated(stacked, kernels, (1, 1), 'VALID', dimension_num...]
    pallas_call x0 -> x3, Pallas kernels: none -> 41.1 us  [the longest x1 15.3 us: finish(): pl.pallas_call(functools.partial(finish_kernel, waves, n), out_shape=jax....]
    dot_general x6 -> x0, matrix products: 30.6 us -> none  [the longest x2 15.9 us: add_group(): jnp.einsum('ibh,ihp->ibp', part_energy, onehot, preferred_element_type=jn...]
    all_to_all x4 -> x0, starting transfers between devices: 18.8 us -> none  [the longest x1 5.23 us: per_device(): lax.all_to_all(send_spot, 'tile', split_axis=0, concat_axis=0, tiled=True)]
    scatter x3 -> x0, local copies, waits for them, and re-layouts: 15.3 us -> none  [the longest x1 12.5 us: per_device(): send_energy = jnp.zeros((tile_count * capacity, band_dev, hit_lanes), hit...]
    ppermute x4 -> x0, starting transfers between devices: 12.5 us -> none  [the longest x2 8.67 us: padded_2(): lax.ppermute(tail, axis, [(i, (i + 1) % count) for i in range(ends)])]
    another operation x3 -> x0, local copies, waits for them, and re-layouts: 11.8 us -> none  [the longest x1 6.27 us: patch_blur(): stacked = pieces.reshape(1, channels, tall, patch_width + 2 * radius)]
    reshape x4 -> x2, local copies, waits for them, and re-layouts: 6.7 us -> 0.24 us  [the longest x1 0.15 us: per_device(): w2 = conv_out.transpose(0, 2, 3, 1).reshape(conv_out.shape[0], -1)]
  transfers between devices with their start and end apart: 8 -> 0, of which waited for: 3 -> 0; matrix products, arithmetic and copies ran while one was open for 19% -> 0% of each run, Pallas kernels for 0% -> 0%
where the time goes in v1:
time: 50.3 us; the launch traced here: 50 us
  Pallas kernels  41.1 us (82%)
  local copies, waits for them, and re-layouts  5.2 us (10%)
  other arithmetic  3.54 us (7%)
    pallas_call x1, Pallas kernels, finish(): pl.pallas_call(functools.partial(finish_kernel, waves, n), out_shape=jax....  15.3 us
    pallas_call x1, Pallas kernels, blur(): pl.pallas_call(functools.partial(blur_kernel, n, cap, scenes, bands), out...  13.7 us
    pallas_call x1, Pallas kernels, dispatch(): pl.pallas_call(functools.partial(dispatch_kernel, n, cap), out_shape=(jax...  12.2 us
    unnamed x11, local copies, waits for them, and re-layouts  4.02 us

profile of v1, /device:TPU:11, one launch (start us, length us, event | category | flops | bytes accessed | tf_op | source)
XLA Modules:
  0.0 50.0 jit_solution(11148451416477743199)
XLA Ops:
  0.0 0.0 copy-start.2
  0.0 0.9 %convert_reduce_fusion = s32[128]{0:T(128)S(1)} fusion(s32[128]{0:T(128)} %bitcast.22), kind=kLoop, calls=%fused_computation.7 | loop fusion | flops 81792 | bytes 1024 | tf_op jit(solution)/shard_map/reduce_sum | solution.py:356
  0.9 0.7 %iota_compare_fusion.3 = pred[8,128]{1,0:T(8,128)(4,1)S(1)} fusion(s32[128]{0:T(128)} %bitcast.23), kind=kLoop, calls=%fused_computation.11 | loop fusion | flops 1024 | bytes 1536 | tf_op jit(solution)/shard_map/eq | solution.py:359
  1.6 0.7 %add_bitcast_fusion = s32[128]{0:T(128)S(1)} fusion(s32[1,128]{1,0:T(1,128)} %param.16, s32[1,128]{1,0:T(1,128)} %param.15), kind=kLoop, calls=%fused_computation.13 | loop fusion | flops 256 | bytes 1536 | tf_op jit(solution)/shard_map/add | solution.py:353
  2.3 0.3 fusion.1
  2.6 0.7 %pad.9 = s32[128]{0:T(128)S(1)} pad(s32[4]{0:T(128)} %bitcast.24, s32[]{:T(128)} %constant.2.clone.1), padding=64_60 | pad | bytes 532 | tf_op jit(solution)/shard_map/jit(_pad)/pad | solution.py:362
  3.4 0.9 %bitcast_select_fusion = s32[128,128]{1,0:T(8,128)S(1)} fusion(s32[1,128,128]{2,1,0:T(8,128)} %param.12, s32[128]{0:T(128)} %bitcast.21), kind=kLoop, calls=%fused_computation.4 | loop fusion | flops 32768 | bytes 131584 | tf_op jit(solution)/shard_map/jit(_where)/select_n | solution.py:365
  4.3 0.0 copy-start.3
  4.4 0.0 copy-start.1
  4.4 0.9 %copy-done.1 = bf16[128,8,128]{2,1,0:T(8,128)(2,1)S(1)} copy-done((bf16[128,8,128]{2,1,0:T(8,128)(2,1)S(1)}, bf16[128,8,128]{2,1,0:T(8,128)(2,1)}, u32[]{:S(2)}) %copy-start.1) | copy-done | bytes 262168
  5.4 12.2 %dispatch.1 = (bf16[8,32,8,128]{3,2,1,0:T(8,128)(2,1)S(1)}, s32[8,32,1,128]{3,2,1,0:T(1,128)S(1)}, s32[8,1,128]{2,1,0:T(1,128)S(1)}) custom-call(s32[8,32]{1,0:T(8,128)S(1)} %bitcast.14, bf16[128,8,128]{2,1,0:T(8,128)(2,1)S(1)} %copy-done.1, s32[129,1,128]{2,1,0:T(1,128)S(1)} %broadcast_in_dim.48.pos_ref, s32[8,1,128]{2,1,0:T(1,128)S(1)} %broadcast_select_fusion.meta_ref), custom_call_target="tpu_custom_call" | custom-call | tf_op jit(solution)/shard_map/dispatch/pallas_call | solution.py:76
  17.6 0.8 %copy.20.resp_ref = f32[32,3]{1,0:T(8,128)S(1)} copy(f32[32,3]{0,1:T(4,128)} %param.19) | data formatting | bytes 768 | tf_op args[8]
  18.3 0.0 copy-start
  18.3 1.6 %copy-done = f32[64,8,961]{2,1,0:T(8,128)S(1)} copy-done((f32[64,8,961]{2,1,0:T(8,128)S(1)}, f32[64,8,961]{2,1,0:T(8,128)}, u32[]{:S(2)}) %copy-start) | copy-done | bytes 1968152
  19.9 13.7 %blur.1.col_ref = f32[4,3,3,16,128]{4,3,2,1,0:T(8,128)S(1)} custom-call(s32[8,128]{1,0:T(8,128)S(1)} %bitcast.15, f32[32,3]{1,0:T(8,128)S(1)} %copy.20.resp_ref, bf16[8,32,8,128]{3,2,1,0:T(8,128)(2,1)S(1)} %get-tuple-element.9.energy_ref, s32[8,32,1,128]{3,2,1,0:T(1,128)S(1)} %get-tuple-element.10.pos_ref, f32[64,8,961]{2,1,0:T(8,128)S(1)} %copy-done), custom_call_target="tpu_custom_call" | custom-call | tf_op jit(solution)/shard_map/blur/pallas_call | solution.py:190
  33.6 0.0 copy-done.2
  33.6 0.1 copy.22
  33.8 0.1 copy.24.w2_ref
  33.9 0.0 copy-done.3
  34.0 0.1 copy.23.w1_ref
  34.0 15.3 %finish.1 = bf16[1,64,16,128]{3,2,1,0:T(8,128)(2,1)S(1)} custom-call(f32[4,3,3,16,128]{4,3,2,1,0:T(8,128)S(1)} %blur.1.col_ref, bf16[64,72]{1,0:T(8,128)(2,1)S(1)} %copy.23.w1_ref, bf16[64,576]{1,0:T(8,128)(2,1)S(1)} %copy.24.w2_ref), custom_call_target="tpu_custom_call" | custom-call | tf_op jit(solution)/shard_map/finish/pallas_call | solution.py:322
  49.3 0.7 %copy.27 = bf16[1,64,16,128]{3,2,1,0:T(8,128)(2,1)} copy(bf16[1,64,16,128]{3,2,1,0:T(8,128)(2,1)S(1)} %finish.1) | data formatting | bytes 524288
  (9 shorter events, 0.1 us)
Async XLA Ops:
  0.0 33.6 %copy-start.2 = (bf16[64,64,3,3]{1,0,3,2:T(8,128)(2,1)S(1)}, bf16[64,64,3,3]{1,0,3,2:T(8,128)(2,1)}, u32[]{:S(2)}) copy-start(bf16[64,64,3,3]{1,0,3,2:T(8,128)(2,1)} %param.21) | copy-start | bytes 221188
  4.3 29.6 %copy-start.3 = (bf16[64,3,3,3]{0,3,2,1:T(4,128)(2,1)S(1)}, bf16[64,3,3,3]{0,3,2,1:T(4,128)(2,1)}, u32[]{:S(2)}) copy-start(bf16[64,3,3,3]{0,3,2,1:T(4,128)(2,1)} %param.20) | copy-start | bytes 10372
  4.4 1.0 %copy-start.1 = (bf16[128,8,128]{2,1,0:T(8,128)(2,1)S(1)}, bf16[128,8,128]{2,1,0:T(8,128)(2,1)}, u32[]{:S(2)}) copy-start(bf16[128,8,128]{2,1,0:T(8,128)(2,1)} %energy_ref.1) | copy-start | bytes 786436
  18.3 1.6 %copy-start = (f32[64,8,961]{2,1,0:T(8,128)S(1)}, f32[64,8,961]{2,1,0:T(8,128)}, u32[]{:S(2)}) copy-start(f32[64,8,961]{2,1,0:T(8,128)} %bank_ref.1) | copy-start | bytes 5904388

commit v2 on v1

v2 whole, which is shorter than its diff:
```python
import functools

import jax
import jax.numpy as jnp
from jax import lax
from jax.experimental import pallas as pl
from jax.experimental.pallas import tpu as pltpu
from jax.sharding import PartitionSpec as P

ROWS = 16
W = 128
WIN = 4
K = 31
RAD = K // 2
PITCH = 32
DEPTH = ROWS * PITCH
MESH = pl.DeviceIdType.MESH
F32 = jnp.float32
BF16 = jnp.bfloat16


def pack_kernel(n, cap, scenes, tile_ref, count_ref, scene_ref, row_ref, index_ref, energy_ref, spot_ref,
                out_e, out_p, out_m, places, used):
    blocks = energy_ref.shape[0]
    halves = out_p.shape[1]
    out_e[...] = jnp.zeros_like(out_e)
    places[...] = jnp.full_like(places, 1023)
    for t in range(n):
        used[t] = 0
        for j in range(cap):
            out_m[t, j] = 0
        for s in range(scenes):
            out_m[t, 64 + s] = index_ref[0, s]
    lane = lax.broadcasted_iota(jnp.int32, (1, W), 1)

    def place(i, carry):
        t = tile_ref[0, i]
        j = used[t]
        used[t] = j + 1
        out_m[t, j] = scene_ref[0, i] * ROWS + row_ref[0, i]
        out_e[t, j] = energy_ref[i]
        places[t, pl.ds(j, 1), :] = jnp.where(lane < count_ref[0, i], spot_ref[0, pl.ds(i, 1), :], 1023)
        return carry

    lax.fori_loop(0, blocks, place, 0, unroll=8)
    step = cap // 2
    if halves == step:
        for t in range(n):
            out_p[t] = places[t, :step] + places[t, step:] * 65536
    else:
        out_p[...] = places[...]


def pack(block_tile, block_count, block_scene, block_row, psf_index, energy, spot, n):
    blocks, bands, lanes = energy.shape
    cap = 2 * blocks // n
    halves = cap // 2 if cap % 16 == 0 else cap
    scenes = psf_index.shape[1]
    vmem = pl.BlockSpec(memory_space=pltpu.VMEM)
    smem = pl.BlockSpec(memory_space=pltpu.SMEM)
    return pl.pallas_call(
        functools.partial(pack_kernel, n, cap, scenes),
        out_shape=(
            jax.ShapeDtypeStruct((n, cap, bands, lanes), energy.dtype),
            jax.ShapeDtypeStruct((n, halves, lanes), jnp.int32),
            jax.ShapeDtypeStruct((n, lanes), jnp.int32),
        ),
        in_specs=[smem] * 5 + [vmem] * 2,
        out_specs=(vmem, vmem, smem),
        scratch_shapes=[pltpu.VMEM((n, cap, lanes), jnp.int32), pltpu.SMEM((n,), jnp.int32)],
        compiler_params=pltpu.CompilerParams(vmem_limit_bytes=63 * 2**20),
        name="pack",
    )(block_tile, block_count, block_scene, block_row, psf_index, energy, spot)


def dispatch_kernel(n, scenes, bands, send_e, send_p, send_m, bank_hbm, got_e, got_p, got_m, toeplitz,
                    bank_ref, index_ref, kpad, amat, send_sem, recv_sem, local_sem):
    wave = lax.axis_index("wave")
    me = lax.axis_index("tile")
    load_bank = pltpu.make_async_copy(bank_hbm, bank_ref, local_sem.at[3])
    load_bank.start()
    barrier = pltpu.get_barrier_semaphore()

    @pl.loop(1, n)
    def _(d):
        pl.semaphore_signal(barrier, inc=1, device_id=(wave, lax.rem(me + d, n)), device_id_type=MESH)

    arrays = ((send_e, got_e), (send_p, got_p), (send_m, got_m))

    def copy_of(k, d):
        peer = lax.rem(me + d, n)
        src, dst = arrays[k]
        return pltpu.make_async_remote_copy(
            src_ref=src.at[peer], dst_ref=dst.at[me], send_sem=send_sem.at[k, d],
            recv_sem=recv_sem.at[k, d], device_id=(wave, peer), device_id_type=MESH)

    own = [pltpu.make_async_copy(src.at[me], dst.at[me], local_sem.at[k]) for k, (src, dst) in enumerate(arrays)]
    for copy in own:
        copy.start()
    pl.semaphore_wait(barrier, n - 1)

    @pl.loop(1, n)
    def _(d):
        copy_of(2, d).start()

    @pl.loop(1, n)
    def _(d):
        copy_of(0, d).start()
        copy_of(1, d).start()

    for copy in own:
        copy.wait()

    @pl.loop(1, n)
    def _(d):
        copy_of(2, d).wait()

    fetch = pltpu.make_async_copy(got_m, index_ref, local_sem.at[4])
    fetch.start()
    fetch.wait()
    load_bank.wait()

    lane = lax.broadcasted_iota(jnp.int32, (bands, W), 1)
    kpad[...] = jnp.zeros_like(kpad)

    def scene_step(s, carry):
        for part in range(3):
            other = jnp.clip(me + part - 1, 0, n - 1)
            flat = bank_ref[index_ref[other, 0, 64 + s]]
            flat = jnp.concatenate([flat, jnp.zeros((bands, 1024 + W - K * K), F32)], axis=1)
            for g in range(8):
                cell = jnp.zeros((bands, W), F32)
                for q in range(4):
                    u = 4 * g + q
                    if u >= K:
                        continue
                    base = K * u // W * W
                    shift = (PITCH * q - (K * u - base)) % (2 * W)
                    piece = flat[:, base:base + 2 * W]
                    if shift:
                        piece = pltpu.roll(piece, shift, 1)
                    hit = (lane >= PITCH * q) & (lane < PITCH * q + K)
                    cell = jnp.where(hit, piece[:, :W], cell)
                kpad[:, 512 + g * W:512 + (g + 1) * W] = cell
            for j in range(ROWS):
                start = 512 + PITCH * (RAD - j + ROWS * (1 - part))
                base = start // W * W
                off = start - base
                piece = kpad[:, base:base + DEPTH + W]
                if off:
                    piece = pltpu.roll(piece, DEPTH + W - off, 1)
                for c4 in range(DEPTH // W):
                    amat[c4, pl.ds(part * ROWS + j, bands, stride=3 * ROWS), :] = (
                        piece[:, c4 * W:(c4 + 1) * W])
        for b in range(bands):
            for c4 in range(DEPTH // W):
                toeplitz[s, b, :, c4 * W:(c4 + 1) * W] = (
                    amat[c4, b * 3 * ROWS:(b + 1) * 3 * ROWS, :].astype(BF16))
        return carry

    lax.fori_loop(0, scenes, scene_step, 0)

    @pl.loop(1, n)
    def _(d):
        copy_of(0, d).wait()
        copy_of(1, d).wait()


def dispatch(energy, pos, meta, bank, scenes):
    n, cap, bands, lanes = energy.shape
    vmem = pl.BlockSpec(memory_space=pltpu.VMEM)
    hbm = pl.BlockSpec(memory_space=pl.ANY)
    return pl.pallas_call(
        functools.partial(dispatch_kernel, n, scenes, bands),
        out_shape=(
            jax.ShapeDtypeStruct(energy.shape, energy.dtype),
            jax.ShapeDtypeStruct(pos.shape, pos.dtype),
            jax.ShapeDtypeStruct(meta.shape, meta.dtype),
            jax.ShapeDtypeStruct((scenes, bands, 3 * ROWS, DEPTH), BF16),
        ),
        in_specs=[hbm] * 4,
        out_specs=(hbm, hbm, hbm, vmem),
        scratch_shapes=[
            pltpu.VMEM(bank.shape, F32),
            pltpu.SMEM(meta.shape, jnp.int32),
            pltpu.VMEM((bands, 2176), F32),
            pltpu.VMEM((DEPTH // W, bands * 3 * ROWS, W), F32),
            pltpu.SemaphoreType.DMA((3, n)),
            pltpu.SemaphoreType.DMA((3, n)),
            pltpu.SemaphoreType.DMA((5,)),
        ],
        compiler_params=pltpu.CompilerParams(
            collective_id=0, has_side_effects=True, vmem_limit_bytes=63 * 2**20),
        name="dispatch",
    )(energy, pos, meta, bank)


def splat_kernel(n, cap, bands, meta_ref, energy_ref, pos_ref, acc):
    group = 8
    halves = pos_ref.shape[1]
    acc[...] = jnp.zeros_like(acc)
    xs = lax.broadcasted_iota(jnp.int32, (W, W), 0)

    def splat_source(d, carry):
        @pl.loop(0, cap // group)
        def _(g):
            windows = []
            for k in range(group):
                j = g * group + k
                if halves == cap:
                    pos = pos_ref[d, pl.ds(j, 1), :]
                else:
                    pos = pos_ref[d, pl.ds(lax.rem(j, halves), 1), :]
                    pos = jnp.where(j < halves, pos & 65535, lax.shift_right_arithmetic(pos, 16))
                row = lax.shift_right_arithmetic(pos, 7)
                col = (W - 1) - (pos & (W - 1))
                onehot = jnp.where(xs == col, 1.0, 0.0).astype(BF16)
                energy = energy_ref[d, j].astype(F32)
                parts = [jnp.where(row == r, energy, 0.0) for r in range(WIN)]
                lhs = jnp.concatenate(parts, axis=0).astype(BF16)
                windows.append(lax.dot_general(
                    lhs, onehot, (((1,), (1,)), ((), ())), preferred_element_type=F32))
            for k in range(group):
                base = pl.multiple_of(meta_ref[d, g * group + k] * bands, bands)
                acc[pl.ds(base, WIN * bands), :] += windows[k]
        return carry

    lax.fori_loop(0, n, splat_source, 0)


def splat(meta, energy, pos, scenes):
    n, cap, bands, lanes = energy.shape
    vmem = pl.BlockSpec(memory_space=pltpu.VMEM)
    smem = pl.BlockSpec(memory_space=pltpu.SMEM)
    return pl.pallas_call(
        functools.partial(splat_kernel, n, cap, bands),
        out_shape=jax.ShapeDtypeStruct((scenes * ROWS * bands, W), F32),
        in_specs=[smem, vmem, vmem],
        out_specs=vmem,
        compiler_params=pltpu.CompilerParams(vmem_limit_bytes=63 * 2**20),
        name="splat",
    )(meta, energy, pos)


def finish_kernel(waves, n, resp_ref, acc, toeplitz, w1_ref, w2_ref, out_ref, col_ref, got, mine, rim, sens, hid, outs,
                  send_sem, recv_sem, rim_send, rim_recv):
    wave = lax.axis_index("wave")
    me = lax.axis_index("tile")
    has_up = me > 0
    has_down = me < n - 1
    barrier = pltpu.get_barrier_semaphore()

    def guarded(part, body):
        if part == 0:
            pl.when(has_up)(body)
        elif part == 2:
            pl.when(has_down)(body)
        else:
            body()

    todo = [(dw, part) for dw in range(waves) for part in range(3) if (dw, part) != (0, 1)]
    for dw, part in todo:
        def greet(dw=dw, part=part):
            pl.semaphore_signal(barrier, inc=1,
                                device_id=(lax.rem(wave + dw, waves), me + part - 1), device_id_type=MESH)
        guarded(part, greet)
    sides = jnp.where(has_up, 1, 0) + jnp.where(has_down, 1, 0)
    pl.semaphore_wait(barrier, waves - 1 + waves * sides)

    def copy_of(dw, part):
        scene = lax.rem(wave + dw, waves)
        return pltpu.make_async_remote_copy(
            src_ref=col_ref.at[scene, part], dst_ref=got.at[dw, part],
            send_sem=send_sem.at[dw, part], recv_sem=recv_sem.at[dw, part],
            device_id=(scene, me + part - 1), device_id_type=MESH)

    bands = toeplitz.shape[1]
    shift_v = lax.broadcasted_iota(jnp.int32, (PITCH, W), 0)
    from_x = lax.broadcasted_iota(jnp.int32, (PITCH, W), 1) - shift_v + RAD
    keep = (from_x >= 0) & (from_x < W) & (shift_v < K)

    def scene_step(i, carry):
        dw = lax.rem(i + 1, waves)
        s = lax.rem(wave + dw, waves)
        colours = [jnp.zeros((3 * ROWS, W), F32) for _ in range(3)]
        for b in range(bands):
            rows = []
            for r in range(ROWS):
                line = acc[pl.ds((s * ROWS + r) * bands + b, 1), :]
                wide = jnp.broadcast_to(line, (PITCH, W))
                wide = pltpu.roll(wide, W - RAD, 1, stride=1, stride_axis=0)
                rows.append(jnp.where(keep, wide, 0.0).astype(BF16))
            rhs = jnp.concatenate(rows, axis=0)
            blurred = jnp.dot(toeplitz[s, b], rhs, preferred_element_type=F32)
            for c in range(3):
                colours[c] = colours[c] + resp_ref[c, wave * bands + b] * blurred
        for part in range(3):
            for c in range(3):
                col_ref[s, part, c] = colours[c][part * ROWS:(part + 1) * ROWS]
        pl.when(has_up)(lambda: copy_of(dw, 0).start())
        pl.when(dw > 0)(lambda: copy_of(dw, 1).start())
        pl.when(has_down)(lambda: copy_of(dw, 2).start())
        return carry

    lax.fori_loop(0, waves, scene_step, 0)

    @pl.when(jnp.logical_not(has_down))
    def _():
        for dw in range(waves):
            got[dw, 0] = jnp.zeros(got.shape[2:], F32)
        rim[1] = jnp.zeros(rim.shape[1:], F32)

    @pl.when(jnp.logical_not(has_up))
    def _():
        for dw in range(waves):
            got[dw, 2] = jnp.zeros(got.shape[2:], F32)
        rim[0] = jnp.zeros(rim.shape[1:], F32)

    for dw, part in todo:
        guarded(2 - part, lambda dw=dw, part=part: copy_of(dw, part).wait_recv())
    total = col_ref[wave, 1]
    for dw, part in todo:
        total = total + got[dw, part]
    sensor = total.astype(BF16)
    flip_r = lax.broadcasted_iota(jnp.int32, (W, W), 0)
    flip_c = lax.broadcasted_iota(jnp.int32, (W, W), 1)
    mirror = jnp.where(flip_r + flip_c == W - 1, 1.0, 0.0).astype(BF16)
    plain = jnp.dot(sensor.reshape(3 * ROWS, W), mirror, preferred_element_type=F32)
    mine[...] = plain.reshape(3, ROWS, W)

    def to_down():
        return pltpu.make_async_remote_copy(
            src_ref=mine.at[:, pl.ds(8, 8)], dst_ref=rim.at[0], send_sem=rim_send.at[0],
            recv_sem=rim_recv.at[0], device_id=(wave, me + 1), device_id_type=MESH)

    def to_up():
        return pltpu.make_async_remote_copy(
            src_ref=mine.at[:, pl.ds(0, 8)], dst_ref=rim.at[1], send_sem=rim_send.at[1],
            recv_sem=rim_recv.at[1], device_id=(wave, me - 1), device_id_type=MESH)

    pl.when(has_down)(lambda: to_down().start())
    pl.when(has_up)(lambda: to_up().start())

    sens[...] = jnp.zeros_like(sens)
    for c in range(3):
        sens[pl.ds(2 * 8 + c, ROWS, stride=8), :] = plain[c * ROWS:(c + 1) * ROWS]
    pl.when(has_up)(lambda: to_down().wait_recv())
    pl.when(has_down)(lambda: to_up().wait_recv())
    for c in range(3):
        for k in range(2):
            sens[pl.ds(k * 8 + c, 1), :] = rim[0, c, 6 + k:7 + k]
            sens[pl.ds((ROWS + 2 + k) * 8 + c, 1), :] = rim[1, c, k:k + 1]

    def shifted(values):
        xs = lax.broadcasted_iota(jnp.int32, values.shape, 1)
        left = jnp.where(xs == 0, 0.0, pltpu.roll(values, 1, 1))
        right = jnp.where(xs == W - 1, 0.0, pltpu.roll(values, W - 1, 1))
        return left, values, right

    spread = jnp.concatenate(
        [jnp.concatenate(shifted(sens[y * 8:(y + 1) * 8, :]), axis=0) for y in range(ROWS + 4)], axis=0
    )
    w1 = w1_ref[...]
    for y in range(ROWS + 2):
        rhs = spread[y * 24:(y + 3) * 24].astype(BF16)
        value = jnp.dot(w1, rhs, preferred_element_type=F32)
        value = value / (1.0 + jnp.exp(-value))
        if y == 0:
            value = jnp.where(has_up, value, 0.0)
        if y == ROWS + 1:
            value = jnp.where(has_down, value, 0.0)
        hid[y] = jnp.concatenate(shifted(value), axis=0).astype(BF16)
    w2 = w2_ref[...]
    channels = w2.shape[0]
    for y in range(ROWS):
        rhs = hid[y:y + 3].reshape(9 * channels, W)
        outs[pl.ds(y, channels, stride=ROWS), :] = jnp.dot(w2, rhs, preferred_element_type=F32)
    out_ref[0] = outs[...].reshape(channels, ROWS, W).astype(BF16)

    for dw, part in todo:
        guarded(part, lambda dw=dw, part=part: copy_of(dw, part).wait_send())
    pl.when(has_down)(lambda: to_down().wait_send())
    pl.when(has_up)(lambda: to_up().wait_send())


def finish(response, acc, toeplitz, w1, w2, waves, n):
    channels = w2.shape[0]
    vmem = pl.BlockSpec(memory_space=pltpu.VMEM)
    return pl.pallas_call(
        functools.partial(finish_kernel, waves, n),
        out_shape=jax.ShapeDtypeStruct((1, channels, ROWS, W), BF16),
        in_specs=[pl.BlockSpec(memory_space=pltpu.SMEM)] + [vmem] * 4,
        out_specs=vmem,
        scratch_shapes=[
            pltpu.VMEM((waves, 3, 3, ROWS, W), F32),
            pltpu.VMEM((waves, 3, 3, ROWS, W), F32),
            pltpu.VMEM((3, ROWS, W), F32),
            pltpu.VMEM((2, 3, 8, W), F32),
            pltpu.VMEM(((ROWS + 4) * 8, W), F32),
            pltpu.VMEM((ROWS + 2, 3 * channels, W), BF16),
            pltpu.VMEM((channels * ROWS, W), F32),
            pltpu.SemaphoreType.DMA((waves, 3)),
            pltpu.SemaphoreType.DMA((waves, 3)),
            pltpu.SemaphoreType.DMA((2,)),
            pltpu.SemaphoreType.DMA((2,)),
        ],
        compiler_params=pltpu.CompilerParams(
            collective_id=1, has_side_effects=True, vmem_limit_bytes=63 * 2**20),
        name="finish",
    )(response, acc, toeplitz, w1, w2)


def per_device(hit_energy, hit_spot, block_tile, block_count, block_scene, block_row, psf_bank,
               psf_index, response, conv_in, conv_out):
    n = lax.axis_size("tile")
    waves = lax.axis_size("wave")
    scenes = psf_index.shape[1]
    blocks = hit_energy.shape[0]
    send_e, send_p, send_m = pack(
        block_tile.reshape(1, blocks), block_count, block_scene, block_row, psf_index.reshape(1, scenes),
        hit_energy, hit_spot, n)
    got_e, got_p, got_m, toeplitz = dispatch(send_e, send_p, send_m[:, None, :], psf_bank, scenes)
    acc = splat(got_m[:, 0, :], got_e, got_p, scenes)
    w1 = jnp.pad(conv_in.transpose(0, 2, 3, 1), ((0, 0), (0, 0), (0, 0), (0, 5))).reshape(-1, 72)
    w2 = conv_out.transpose(0, 2, 3, 1).reshape(conv_out.shape[0], -1)
    return finish(response.T, acc, toeplitz, w1, w2, waves, n)


def solution(mesh):
    in_specs = (
        P("tile", "wave", None),
        P("wave", "tile", None),
        P("wave", "tile", None),
        P("wave", "tile"),
        P("wave", "tile"),
        P("wave", "tile"),
        P(None, "wave", None),
        P("tile", None, None),
        P(),
        P(),
        P(),
    )
    out_specs = P("wave", None, "tile", None)
    return jax.shard_map(
        per_device, mesh=mesh, in_specs=in_specs, out_specs=out_specs, check_vma=False
    )
```

time: 50.3 us -> 47.7 us (0.948)
  other arithmetic: 3.54 us -> 0 us
  Pallas kernels: 41.1 us -> 44.1 us
  local copies, waits for them, and re-layouts: 5.2 us -> 3.31 us
    pallas_call x1, Pallas kernels: 15.3 us -> 18.5 us  [finish(): pl.pallas_call(functools.partial(finish_kernel, waves, n), out_shape=jax....]
    unnamed x11 -> x6, local copies, waits for them, and re-layouts: 4.02 us -> 1.69 us
    reduce_sum x2 -> x0, other arithmetic: 1.24 us -> none  [the longest x1 0.9 us: per_device(): rank = jnp.sum(same.astype(jnp.int32), axis=1)]
    select_n x2 -> x0, other arithmetic: 0.93 us -> none  [the longest x1 0.92 us: per_device(): pos = jnp.where(live, hit_spot[0], -1)]
    pad x1 -> x0, local copies, waits for them, and re-layouts: 0.73 us -> none  [per_device(): psf_row = jnp.pad(psf_index[0, :, 0], (64, lanes - 64 - scenes))]
    eq x2 -> x0, other arithmetic: 0.69 us -> none  [the longest x1 0.66 us: per_device(): target[None, None, :] == tiles[:, None, None]]
    add x2 -> x0, other arithmetic: 0.68 us -> none  [the longest x1 0.67 us: per_device(): base = block_scene[0] * ROWS + block_row[0]]
    reshape x1, local copies, waits for them, and re-layouts: 0.15 us -> 0.77 us  [per_device(): w2 = conv_out.transpose(0, 2, 3, 1).reshape(conv_out.shape[0], -1)]
where the time goes in v2:
time: 47.7 us; the launch traced here: 47.4 us
  Pallas kernels  44.1 us (92%)
  local copies, waits for them, and re-layouts  3.31 us (7%)
    pallas_call x1, Pallas kernels, finish(): pl.pallas_call(functools.partial(finish_kernel, waves, n), out_shape=jax....  18.5 us
    pallas_call x1, Pallas kernels, dispatch(): pl.pallas_call(functools.partial(dispatch_kernel, n, scenes, bands), out_...  12.4 us
    pallas_call x1, Pallas kernels, splat(): pl.pallas_call(functools.partial(splat_kernel, n, cap, bands), out_shape=...  10.3 us
    pallas_call x1, Pallas kernels, pack(): pl.pallas_call(functools.partial(pack_kernel, n, cap, scenes), out_shape=...  2.91 us
    unnamed x6, local copies, waits for them, and re-layouts  1.69 us

profile of v2, /device:TPU:11, one launch (start us, length us, event | category | flops | bytes accessed | tf_op | source)
XLA Modules:
  0.0 47.4 jit_solution(9202947998551814344)
XLA Ops:
  0.0 0.0 copy-start
  0.0 2.9 %pack.1 = (bf16[8,32,8,128]{3,2,1,0:T(8,128)(2,1)}, s32[8,16,128]{2,1,0:T(8,128)}, s32[8,128]{1,0:T(8,128)}) custom-call(s32[1,128]{1,0:T(1,128)} %bitcast.16, s32[1,128]{1,0:T(1,128)} %count_ref.1, s32[1,128]{1,0:T(1,128)} %scene_ref.1, s32[1,128]{1,0:T(1,128)} %row_ref.1, s32[1,4]{1,0:T(1,128)} %bitcast.17, bf16[128,8,128]{2,1,0:T(8,128)(2,1)} %energy_ref.1, ...), custom_call_target="tpu_custom_call" | custom-call | tf_op jit(solution)/shard_map/pack/pallas_call | solution.py:61
  2.9 0.0 copy-start.1
  2.9 12.4 %dispatch.1 = (bf16[8,32,8,128]{3,2,1,0:T(8,128)(2,1)}, s32[8,16,128]{2,1,0:T(8,128)}, s32[8,1,128]{2,1,0:T(1,128)}, bf16[4,8,48,512]{3,2,1,0:T(8,128)(2,1)}) custom-call(bf16[8,32,8,128]{3,2,1,0:T(8,128)(2,1)} %get-tuple-element.12.send_e, s32[8,16,128]{2,1,0:T(8,128)} %get-tuple-element.13.send_p, s32[8,1,128]{2,1,0:T(1,128)} %bitcast.13, ...), custom_call_target="tpu_custom_call" | custom-call | tf_op jit(solution)/shard_map/dispatch/pallas_call | solution.py:173
  15.3 10.3 %splat.1.acc = f32[512,128]{1,0:T(8,128)} custom-call(s32[8,128]{1,0:T(8,128)} %bitcast.14, bf16[8,32,8,128]{3,2,1,0:T(8,128)(2,1)} %get-tuple-element.16.energy_ref, s32[8,16,128]{2,1,0:T(8,128)} %get-tuple-element.17.pos_ref), custom_call_target="tpu_custom_call" | custom-call | tf_op jit(solution)/shard_map/splat/pallas_call | solution.py:235
  25.6 0.0 copy-done
  25.6 0.1 copy.15
  25.7 0.8 %copy.17.w2_ref = bf16[64,576]{1,0:T(8,128)(2,1)} copy(bf16[64,576]{0,1:T(8,128)(2,1)S(1)} %bitcast.9) | data formatting | bytes 147456 | tf_op jit(solution)/shard_map/reshape | solution.py:425
  26.5 0.0 copy-done.1
  26.5 0.7 %copy.16.w1_ref = bf16[64,72]{1,0:T(8,128)(2,1)} copy(bf16[64,72]{0,1:T(8,128)(2,1)S(1)} %bitcast.11) | data formatting | bytes 18432 | tf_op jit(solution)/shard_map/reshape | solution.py:424
  27.2 18.5 %finish.1 = bf16[1,64,16,128]{3,2,1,0:T(8,128)(2,1)} custom-call(f32[3,32]{1,0:T(4,128)} %bitcast.15, f32[512,128]{1,0:T(8,128)} %splat.1.acc, bf16[4,8,48,512]{3,2,1,0:T(8,128)(2,1)} %get-tuple-element.18.toeplitz, bf16[64,72]{1,0:T(8,128)(2,1)} %copy.16.w1_ref, bf16[64,576]{1,0:T(8,128)(2,1)} %copy.17.w2_ref), custom_call_target="tpu_custom_call" | custom-call | tf_op jit(solution)/shard_map/finish/pallas_call | solution.py:389
  45.8 1.7 %copy.20 = bf16[1,64,16,128]{3,2,1,0:T(8,128)(2,1)} copy(bf16[1,64,16,128]{3,2,1,0:T(8,128)(2,1)} %finish.1) | data formatting | bytes 524288
  (2 shorter events, 0.0 us)
Async XLA Ops:
  0.0 25.6 %copy-start = (bf16[64,64,3,3]{1,0,3,2:T(8,128)(2,1)S(1)}, bf16[64,64,3,3]{1,0,3,2:T(8,128)(2,1)}, u32[]{:S(2)}) copy-start(bf16[64,64,3,3]{1,0,3,2:T(8,128)(2,1)} %param.21) | copy-start | bytes 221188
  2.9 23.6 %copy-start.1 = (bf16[64,3,3,3]{0,3,2,1:T(4,128)(2,1)S(1)}, bf16[64,3,3,3]{0,3,2,1:T(4,128)(2,1)}, u32[]{:S(2)}) copy-start(bf16[64,3,3,3]{0,3,2,1:T(4,128)(2,1)} %param.20) | copy-start | bytes 10372

commit v3 on v2

--- a/solution.py
+++ b/solution.py
@@ -1,4 +1,5 @@
 import functools
+import math
 
 import jax
 import jax.numpy as jnp
@@ -196,7 +197,7 @@
 
 
 def splat_kernel(n, cap, bands, meta_ref, energy_ref, pos_ref, acc):
-    group = 8
+    group = math.gcd(cap, 32)
     halves = pos_ref.shape[1]
     acc[...] = jnp.zeros_like(acc)
     xs = lax.broadcasted_iota(jnp.int32, (W, W), 0)

time: 47.7 us -> 44.7 us (0.937)
  Pallas kernels: 44.1 us -> 41.1 us
    pallas_call x1, Pallas kernels: 10.3 us -> 7.22 us  [splat(): pl.pallas_call(functools.partial(splat_kernel, n, cap, bands), out_shape=...]
where the time goes in v3:
time: 44.7 us; the launch traced here: 44.5 us
  Pallas kernels  41.1 us (92%)
  local copies, waits for them, and re-layouts  3.31 us (7%)
    pallas_call x1, Pallas kernels, finish(): pl.pallas_call(functools.partial(finish_kernel, waves, n), out_shape=jax....  18.6 us
    pallas_call x1, Pallas kernels, dispatch(): pl.pallas_call(functools.partial(dispatch_kernel, n, scenes, bands), out_...  12.4 us
    pallas_call x1, Pallas kernels, splat(): pl.pallas_call(functools.partial(splat_kernel, n, cap, bands), out_shape=...  7.22 us
    pallas_call x1, Pallas kernels, pack(): pl.pallas_call(functools.partial(pack_kernel, n, cap, scenes), out_shape=...  2.91 us
    unnamed x6, local copies, waits for them, and re-layouts  1.69 us

profile of v3, /device:TPU:11, one launch (start us, length us, event | category | flops | bytes accessed | tf_op | source)
XLA Modules:
  0.0 44.5 jit_solution(16447456583642558041)
XLA Ops:
  0.0 0.0 copy-start
  0.0 2.9 %pack.1 = (bf16[8,32,8,128]{3,2,1,0:T(8,128)(2,1)}, s32[8,16,128]{2,1,0:T(8,128)}, s32[8,128]{1,0:T(8,128)}) custom-call(s32[1,128]{1,0:T(1,128)} %bitcast.16, s32[1,128]{1,0:T(1,128)} %count_ref.1, s32[1,128]{1,0:T(1,128)} %scene_ref.1, s32[1,128]{1,0:T(1,128)} %row_ref.1, s32[1,4]{1,0:T(1,128)} %bitcast.17, bf16[128,8,128]{2,1,0:T(8,128)(2,1)} %energy_ref.1, ...), custom_call_target="tpu_custom_call" | custom-call | tf_op jit(solution)/shard_map/pack/pallas_call | solution.py:62
  2.9 0.0 copy-start.1
  2.9 12.4 %dispatch.1 = (bf16[8,32,8,128]{3,2,1,0:T(8,128)(2,1)}, s32[8,16,128]{2,1,0:T(8,128)}, s32[8,1,128]{2,1,0:T(1,128)}, bf16[4,8,48,512]{3,2,1,0:T(8,128)(2,1)}) custom-call(bf16[8,32,8,128]{3,2,1,0:T(8,128)(2,1)} %get-tuple-element.12.send_e, s32[8,16,128]{2,1,0:T(8,128)} %get-tuple-element.13.send_p, s32[8,1,128]{2,1,0:T(1,128)} %bitcast.13, ...), custom_call_target="tpu_custom_call" | custom-call | tf_op jit(solution)/shard_map/dispatch/pallas_call | solution.py:174
  15.3 7.2 %splat.1.acc = f32[512,128]{1,0:T(8,128)} custom-call(s32[8,128]{1,0:T(8,128)} %bitcast.14, bf16[8,32,8,128]{3,2,1,0:T(8,128)(2,1)} %get-tuple-element.16.energy_ref, s32[8,16,128]{2,1,0:T(8,128)} %get-tuple-element.17.pos_ref), custom_call_target="tpu_custom_call" | custom-call | tf_op jit(solution)/shard_map/splat/pallas_call | solution.py:236
  22.5 0.0 copy-done
  22.5 0.1 copy.15
  22.7 0.8 %copy.17.w2_ref = bf16[64,576]{1,0:T(8,128)(2,1)} copy(bf16[64,576]{0,1:T(8,128)(2,1)S(1)} %bitcast.9) | data formatting | bytes 147456 | tf_op jit(solution)/shard_map/reshape | solution.py:426
  23.4 0.0 copy-done.1
  23.5 0.7 %copy.16.w1_ref = bf16[64,72]{1,0:T(8,128)(2,1)} copy(bf16[64,72]{0,1:T(8,128)(2,1)S(1)} %bitcast.11) | data formatting | bytes 18432 | tf_op jit(solution)/shard_map/reshape | solution.py:425
  24.2 18.6 %finish.1 = bf16[1,64,16,128]{3,2,1,0:T(8,128)(2,1)} custom-call(f32[3,32]{1,0:T(4,128)} %bitcast.15, f32[512,128]{1,0:T(8,128)} %splat.1.acc, bf16[4,8,48,512]{3,2,1,0:T(8,128)(2,1)} %get-tuple-element.18.toeplitz, bf16[64,72]{1,0:T(8,128)(2,1)} %copy.16.w1_ref, bf16[64,576]{1,0:T(8,128)(2,1)} %copy.17.w2_ref), custom_call_target="tpu_custom_call" | custom-call | tf_op jit(solution)/shard_map/finish/pallas_call | solution.py:390
  42.8 1.7 %copy.20 = bf16[1,64,16,128]{3,2,1,0:T(8,128)(2,1)} copy(bf16[1,64,16,128]{3,2,1,0:T(8,128)(2,1)} %finish.1) | data formatting | bytes 524288
  (2 shorter events, 0.0 us)
Async XLA Ops:
  0.0 22.5 %copy-start = (bf16[64,64,3,3]{1,0,3,2:T(8,128)(2,1)S(1)}, bf16[64,64,3,3]{1,0,3,2:T(8,128)(2,1)}, u32[]{:S(2)}) copy-start(bf16[64,64,3,3]{1,0,3,2:T(8,128)(2,1)} %param.21) | copy-start | bytes 221188
  2.9 20.5 %copy-start.1 = (bf16[64,3,3,3]{0,3,2,1:T(4,128)(2,1)S(1)}, bf16[64,3,3,3]{0,3,2,1:T(4,128)(2,1)}, u32[]{:S(2)}) copy-start(bf16[64,3,3,3]{0,3,2,1:T(4,128)(2,1)} %param.20) | copy-start | bytes 10372
